TPU v7x, 512 devices: a whole 4x8x8 slice. The times are simulated.
512 devices in a mesh: sx: 32 (over y_lo, x, core), sy: 16 (over z, y_hi).
Axes of the slice: x: 4, y: 8 (y_hi: 2, y_lo: 4; y = y_hi * 4 + y_lo), z: 8, core: 2. Of those that a mesh axis runs over, the one named last changes fastest.
Arguments:
- schur_x: float32 [64, 16, 512, 512], P('sx', 'sy'), may hold values from -1 to 5, as said below
- schur_y: float32 [32, 32, 512, 512], P('sx', 'sy'), may hold values from -1 to 5, as said below
- residual_x: float32 [64, 16, 32, 512], P('sx', 'sy'), may hold values from -36 to 36
- residual_y: float32 [32, 32, 32, 512], P('sx', 'sy'), may hold values from -36 to 36
- basis_x: float32 [64, 16, 6, 512], P('sx', 'sy'), may hold values from -0.9 to 0.9
- basis_y: float32 [32, 32, 6, 512], P('sx', 'sy'), may hold values from -0.9 to 0.9
- couple_x: float32 [32, 16, 6, 6], P('sx', 'sy'), may hold values from -0.3 to 0.1
- couple_y: float32 [32, 16, 6, 6], P('sx', 'sy'), may hold values from -0.3 to 0.1
- coarse_shift: float32 [32, 16, 6], P('sx', 'sy'), may hold values from 0.05 to 0.5
Outputs:
- average_x: float32 [64, 16, 32, 512], P('sx', 'sy')
- average_y: float32 [32, 32, 32, 512], P('sx', 'sy')
- coarse_values: float32 [32, 16, 6, 32], P('sx', 'sy')
Inputs may be any that keep to these rules, and one draw needn't show every extreme that they name: `schur_x`: every block is symmetric positive definite. `schur_y`: every block is symmetric positive definite.
All inputs are finite; a program needn't handle non-finite values.
Results may differ from a plain program's by a relative error of at most 0.0003.
Values sent between devices are 32-bit elements; how exact they have to be, the bound alone decides.
A program may use at most 128 MiB of HBM per device.

v0:
```python
import jax
import jax.numpy as jnp
from jax import lax
from jax.sharding import PartitionSpec as P

CITERS = 8


HIGH = lax.Precision.HIGHEST


def shifted(array, axis, by):
    count = lax.axis_size(axis)
    pairs = [(i, i + by) for i in range(count) if 0 <= i + by < count]
    return lax.ppermute(array, axis, pairs)


def with_halo(cells, sides, width):
    for axis, dim in sides:
        count = lax.axis_size(axis)
        ends = count - 1
        head = lax.slice_in_dim(cells, 0, width, axis=dim)
        tail = lax.slice_in_dim(cells, cells.shape[dim] - width, cells.shape[dim], axis=dim)
        cells = jnp.concatenate(
            [
                lax.ppermute(tail, axis, [(i, (i + 1) % count) for i in range(ends)]),
                cells,
                lax.ppermute(head, axis, [((i + 1) % count, i) for i in range(ends)]),
            ],
            axis=dim,
        )
    return cells


def face_average(s_low, s_high, r_low, r_high):
    summed = s_low + s_high
    factor = jnp.linalg.cholesky(summed)
    right_side = jnp.dot(s_low, r_low.T, precision=HIGH) + jnp.dot(s_high, r_high.T, precision=HIGH)
    forward = jax.scipy.linalg.solve_triangular(factor, right_side, lower=True)
    solved = jax.scipy.linalg.solve_triangular(factor, forward, lower=True, trans=1)
    return solved.T


def shards(
    schur_x, schur_y, residual_x, residual_y, basis_x, basis_y, couple_x, couple_y, coarse_shift
):
    row_index = lax.axis_index("sx")
    row_count = lax.axis_size("sx")
    col_index = lax.axis_index("sy")
    col_count = lax.axis_size("sy")
    link_x = couple_x[0, 0] * (row_index > 0).astype(jnp.float32)
    link_y = couple_y[0, 0] * (col_index > 0).astype(jnp.float32)
    below_x = shifted((schur_x[1, 0], residual_x[1, 0]), "sx", 1)
    above_x = shifted((schur_x[0, 0], residual_x[0, 0], link_x), "sx", -1)
    below_y = shifted((schur_y[0, 1], residual_y[0, 1]), "sy", 1)
    above_y = shifted((schur_y[0, 0], residual_y[0, 0], link_y), "sy", -1)
    lower_x = face_average(below_x[0], schur_x[0, 0], below_x[1], residual_x[0, 0])
    upper_x = face_average(schur_x[1, 0], above_x[0], residual_x[1, 0], above_x[1])
    lower_y = face_average(below_y[0], schur_y[0, 0], below_y[1], residual_y[0, 0])
    upper_y = face_average(schur_y[0, 1], above_y[0], residual_y[0, 1], above_y[1])
    next_x = above_x[2]
    next_y = above_y[2]
    lower_x = jnp.where(row_index == 0, residual_x[0, 0], lower_x)
    upper_x = jnp.where(row_index == row_count - 1, residual_x[1, 0], upper_x)
    lower_y = jnp.where(col_index == 0, residual_y[0, 0], lower_y)
    upper_y = jnp.where(col_index == col_count - 1, residual_y[0, 1], upper_y)
    rhs_coarse = jnp.einsum("spf,srf->pr", basis_x[:, 0], residual_x[:, 0], precision=HIGH)
    rhs_coarse = rhs_coarse + jnp.einsum("spf,srf->pr", basis_y[0], residual_y[0], precision=HIGH)
    diagonal = (
        jnp.sum(jnp.abs(link_x), axis=0)
        + jnp.sum(jnp.abs(next_x), axis=1)
        + jnp.sum(jnp.abs(link_y), axis=0)
        + jnp.sum(jnp.abs(next_y), axis=1)
        + coarse_shift[0, 0]
    )
    coarse = jnp.zeros_like(rhs_coarse)
    remain = rhs_coarse

    def squares(values):
        return lax.psum(jnp.sum(values * values, axis=0), ("sx", "sy"))

    direction = rhs_coarse
    norm_now = squares(remain)
    for sweep_index in range(CITERS):
        padded = with_halo(direction[None, None], (("sx", 0), ("sy", 1)), 1)
        image = diagonal[:, None] * direction
        image = image + jnp.dot(link_x.T, padded[0, 1], precision=HIGH)
        image = image + jnp.dot(next_x, padded[2, 1], precision=HIGH)
        image = image + jnp.dot(link_y.T, padded[1, 0], precision=HIGH)
        image = image + jnp.dot(next_y, padded[1, 2], precision=HIGH)
        curve = lax.psum(jnp.sum(direction * image, axis=0), ("sx", "sy"))
        alpha = norm_now / curve
        coarse = coarse + alpha * direction
        remain = remain - alpha * image
        norm_next = squares(remain)
        direction = remain + norm_next / norm_now * direction
        norm_now = norm_next
    lift_x = jnp.einsum("pr,spf->srf", coarse, basis_x[:, 0], precision=HIGH)
    lift_y = jnp.einsum("pr,spf->srf", coarse, basis_y[0], precision=HIGH)
    out_x = (jnp.stack([lower_x, upper_x], axis=0) + lift_x)[:, None]
    out_y = (jnp.stack([lower_y, upper_y], axis=0) + lift_y)[None]
    return (out_x, out_y, coarse[None, None])


def solution(mesh):
    placed = (
        P("sx", "sy", None, None),
        P("sx", "sy", None, None),
        P("sx", "sy", None, None),
        P("sx", "sy", None, None),
        P("sx", "sy", None, None),
        P("sx", "sy", None, None),
        P("sx", "sy", None, None),
        P("sx", "sy", None, None),
        P("sx", "sy", None),
    )
    return jax.shard_map(
        shards,
        mesh=mesh,
        in_specs=placed,
        out_specs=(P("sx", "sy", None, None), P("sx", "sy", None, None), P("sx", "sy", None, None)),
        check_vma=False,
    )
```

profile of v0, /device:TPU:66, one launch (start us, length us, event | category | flops | bytes accessed | tf_op | source)
XLA Modules:
  0.0 2324.2 jit_solution(16223693384827084530)
XLA Ops:
  52.2 110.4 %all-reduce.1 = (f32[32]{0:T(128)S(1)}, f32[32]{0:T(128)S(1)}) all-reduce(f32[32]{0:T(128)S(1)} %get-tuple-element.73, f32[32]{0:T(128)S(1)} %get-tuple-element.72), channel_id=1, replica_groups=mesh['sx'=32,'sy'=16] {'sx','sy'}, use_global_device_ids=true, to_apply=%region_9.13 | all-reduce | flops 64 | bytes 512 | tf_op jit(solution)/shard_map/psum | solution.py:80
  165.9 94.4 %psum.114 = f32[32]{0:T(128)S(1)} all-reduce(f32[32]{0:T(128)S(1)} %multiply_reduce_fusion.12), channel_id=1, replica_groups=mesh['sx'=32,'sy'=16] {'sx','sy'}, use_global_device_ids=true, to_apply=%region_17.21 | all-reduce | flops 32 | bytes 256 | tf_op jit(solution)/shard_map/psum | solution.py:80
  283.4 96.4 %psum.115 = f32[32]{0:T(128)S(1)} all-reduce(f32[32]{0:T(128)S(1)} %get-tuple-element.183), channel_id=1, replica_groups=mesh['sx'=32,'sy'=16] {'sx','sy'}, use_global_device_ids=true, to_apply=%region_19.23 | all-reduce | flops 32 | bytes 256 | tf_op jit(solution)/shard_map/psum | solution.py:91
  379.9 95.0 %psum.116 = f32[32]{0:T(128)S(1)} all-reduce(f32[32]{0:T(128)S(1)} %get-tuple-element.116), channel_id=1, replica_groups=mesh['sx'=32,'sy'=16] {'sx','sy'}, use_global_device_ids=true, to_apply=%region_21.25 | all-reduce | flops 32 | bytes 256 | tf_op jit(solution)/shard_map/psum | solution.py:80
  498.2 97.0 %psum.117 = f32[32]{0:T(128)S(1)} all-reduce(f32[32]{0:T(128)S(1)} %get-tuple-element.185), channel_id=1, replica_groups=mesh['sx'=32,'sy'=16] {'sx','sy'}, use_global_device_ids=true, to_apply=%region_23.27 | all-reduce | flops 32 | bytes 256 | tf_op jit(solution)/shard_map/psum | solution.py:91
  595.2 95.0 %psum.118 = f32[32]{0:T(128)S(1)} all-reduce(f32[32]{0:T(128)S(1)} %get-tuple-element.114), channel_id=1, replica_groups=mesh['sx'=32,'sy'=16] {'sx','sy'}, use_global_device_ids=true, to_apply=%region_25.29 | all-reduce | flops 32 | bytes 256 | tf_op jit(solution)/shard_map/psum | solution.py:80
  713.7 97.1 %psum.119 = f32[32]{0:T(128)S(1)} all-reduce(f32[32]{0:T(128)S(1)} %get-tuple-element.187), channel_id=1, replica_groups=mesh['sx'=32,'sy'=16] {'sx','sy'}, use_global_device_ids=true, to_apply=%region_27.31 | all-reduce | flops 32 | bytes 256 | tf_op jit(solution)/shard_map/psum | solution.py:91
  810.8 95.5 %psum.120 = f32[32]{0:T(128)S(1)} all-reduce(f32[32]{0:T(128)S(1)} %get-tuple-element.112), channel_id=1, replica_groups=mesh['sx'=32,'sy'=16] {'sx','sy'}, use_global_device_ids=true, to_apply=%region_29.33 | all-reduce | flops 32 | bytes 256 | tf_op jit(solution)/shard_map/psum | solution.py:80
  929.6 97.1 %psum.121 = f32[32]{0:T(128)S(1)} all-reduce(f32[32]{0:T(128)S(1)} %get-tuple-element.189), channel_id=1, replica_groups=mesh['sx'=32,'sy'=16] {'sx','sy'}, use_global_device_ids=true, to_apply=%region_31.35 | all-reduce | flops 32 | bytes 256 | tf_op jit(solution)/shard_map/psum | solution.py:91
  1026.7 95.1 %psum.122 = f32[32]{0:T(128)S(1)} all-reduce(f32[32]{0:T(128)S(1)} %get-tuple-element.110), channel_id=1, replica_groups=mesh['sx'=32,'sy'=16] {'sx','sy'}, use_global_device_ids=true, to_apply=%region_33.37 | all-reduce | flops 32 | bytes 256 | tf_op jit(solution)/shard_map/psum | solution.py:80
  1145.8 97.0 %psum.123 = f32[32]{0:T(128)S(1)} all-reduce(f32[32]{0:T(128)S(1)} %get-tuple-element.191), channel_id=1, replica_groups=mesh['sx'=32,'sy'=16] {'sx','sy'}, use_global_device_ids=true, to_apply=%region_35.39 | all-reduce | flops 32 | bytes 256 | tf_op jit(solution)/shard_map/psum | solution.py:91
  1242.9 95.0 %psum.124 = f32[32]{0:T(128)S(1)} all-reduce(f32[32]{0:T(128)S(1)} %get-tuple-element.108), channel_id=1, replica_groups=mesh['sx'=32,'sy'=16] {'sx','sy'}, use_global_device_ids=true, to_apply=%region_37.41 | all-reduce | flops 32 | bytes 256 | tf_op jit(solution)/shard_map/psum | solution.py:80
  1361.9 97.1 %psum.125 = f32[32]{0:T(128)S(1)} all-reduce(f32[32]{0:T(128)S(1)} %get-tuple-element.193), channel_id=1, replica_groups=mesh['sx'=32,'sy'=16] {'sx','sy'}, use_global_device_ids=true, to_apply=%region_39.43 | all-reduce | flops 32 | bytes 256 | tf_op jit(solution)/shard_map/psum | solution.py:91
  1459.0 95.0 %psum.126 = f32[32]{0:T(128)S(1)} all-reduce(f32[32]{0:T(128)S(1)} %multiply_reduce_fusion), channel_id=1, replica_groups=mesh['sx'=32,'sy'=16] {'sx','sy'}, use_global_device_ids=true, to_apply=%region_41.45 | all-reduce | flops 32 | bytes 256 | tf_op jit(solution)/shard_map/psum | solution.py:80
  1590.9 131.7 %psum.127 = f32[32]{0:T(128)S(1)} all-reduce(f32[32]{0:T(128)S(1)} %fusion.30), channel_id=1, replica_groups=mesh['sx'=32,'sy'=16] {'sx','sy'}, use_global_device_ids=true, to_apply=%region_43.47 | all-reduce | flops 32 | bytes 256 | tf_op jit(solution)/shard_map/psum | solution.py:91
  1732.6 11.7 cholesky.462
  1744.5 9.8 custom-call.41
  1756.8 11.7 cholesky.481
  1768.6 10.2 custom-call.42
  1780.4 11.7 cholesky.502
  1792.1 9.8 custom-call.43
  1803.4 11.7 cholesky.519
  1827.8 39.3 %custom-call.45 = f32[4,128,128]{1,2,0:T(8,128)S(1)} custom-call(f32[4,128,128]{2,1,0:T(8,128)S(1)} %get-tuple-element.59), custom_call_target="InvertDiagBlocksLowerTriangular" | custom-call | tf_op jit(solution)/shard_map/jit(_solve_triangular)/triangular_solve | solution.py:40
  1889.2 11.7 cholesky.534
  1901.1 9.8 custom-call.46
  1913.4 11.7 cholesky.553
  1925.2 10.2 custom-call.47
  1936.9 11.7 cholesky.574
  1948.7 9.8 custom-call.48
  1960.0 11.7 cholesky.591
  1977.4 11.0 while.17
  1990.0 40.7 %custom-call.50 = f32[4,128,128]{1,2,0:T(8,128)} custom-call(f32[4,128,128]{2,1,0:T(8,128)} %get-tuple-element.61), custom_call_target="InvertDiagBlocksLowerTriangular" | custom-call | tf_op jit(solution)/shard_map/jit(_solve_triangular)/triangular_solve | solution.py:40
  2042.4 11.7 cholesky.606
  2054.2 9.8 custom-call.51
  2064.7 12.1 cholesky.625
  2076.9 9.8 custom-call.52
  2087.3 11.7 cholesky.646
  2099.1 9.8 custom-call.53
  2109.5 11.9 cholesky.663
  2135.7 39.3 %custom-call.55 = f32[4,128,128]{1,2,0:T(8,128)S(1)} custom-call(f32[4,128,128]{2,1,0:T(8,128)S(1)} %get-tuple-element.63), custom_call_target="InvertDiagBlocksLowerTriangular" | custom-call | tf_op jit(solution)/shard_map/jit(_solve_triangular)/triangular_solve | solution.py:40
  2184.5 11.7 cholesky.678
  2196.4 9.8 custom-call.56
  2206.9 11.9 cholesky.697
  2218.8 9.8 custom-call.57
  2229.3 11.7 cholesky.718
  2241.1 9.8 custom-call.58
  2251.5 12.1 cholesky.735
  2277.6 39.3 %custom-call.60 = f32[4,128,128]{1,2,0:T(8,128)S(1)} custom-call(f32[4,128,128]{2,1,0:T(8,128)S(1)} %get-tuple-element.65), custom_call_target="InvertDiagBlocksLowerTriangular" | custom-call | tf_op jit(solution)/shard_map/jit(_solve_triangular)/triangular_solve | solution.py:40
  (455 shorter events, 379.9 us)
Async XLA Ops:
  3.7 30.2 %collective-permute-start.7 = (f32[1,1,6,32]{3,2,1,0:T(8,128)S(1)}, f32[1,1,6,32]{3,2,1,0:T(8,128)S(1)}, u32[]{:S(2)}, u32[]{:S(2)}) collective-permute-start(f32[1,1,6,32]{3,2,1,0:T(8,128)S(1)} %bitcast.543), channel_id=1, source_target_pairs={{16,0},{32,16},{48,32},{64,48},{80,64},{96,80},{112,96},{128,112},... | collective-permute-start | bytes 2312 | tf_op jit(solution)/shard_map/ppermute | solution.py:28
  5.6 28.3 %collective-permute-start.6 = (f32[1,1,6,32]{3,2,1,0:T(8,128)S(1)}, f32[1,1,6,32]{3,2,1,0:T(8,128)S(1)}, u32[]{:S(2)}, u32[]{:S(2)}) collective-permute-start(f32[1,1,6,32]{3,2,1,0:T(8,128)S(1)} %bitcast.544), channel_id=1, source_target_pairs={{0,16},{16,32},{32,48},{48,64},{64,80},{80,96},{96,112},{112,128},... | collective-permute-start | bytes 2312 | tf_op jit(solution)/shard_map/ppermute | solution.py:26
  11.1 1712.1 %collective-permute-start = (f32[512,512]{0,1:T(8,128)}, f32[512,512]{0,1:T(8,128)}, u32[]{:S(2)}, u32[]{:S(2)}) collective-permute-start(f32[512,512]{0,1:T(8,128)} %bitcast.1), channel_id=1, source_target_pairs={{0,16},{16,32},{32,48},{48,64},{64,80},{80,96},{96,112},{112,128},... | collective-permute-start | bytes 3145736 | tf_op jit(solution)/shard_map/ppermute | solution.py:15
  14.8 1852.4 %collective-permute-start.1 = (f32[32,512]{1,0:T(8,128)}, f32[32,512]{1,0:T(8,128)}, u32[]{:S(2)}, u32[]{:S(2)}) collective-permute-start(f32[32,512]{1,0:T(8,128)} %get-tuple-element.136), channel_id=1, source_target_pairs={{0,16},{16,32},{32,48},{48,64},{64,80},{80,96},{96,112},{112,128},... | collective-permute-start | bytes 196616 | tf_op jit(solution)/shard_map/ppermute | solution.py:15
  17.2 9.4 collective-permute-start.5
  26.6 3.5 collective-permute-start.4
  30.1 1846.8 %collective-permute-start.2 = (f32[512,512]{0,1:T(8,128)}, f32[512,512]{0,1:T(8,128)S(1)}, u32[]{:S(2)}, u32[]{:S(2)}) collective-permute-start(f32[512,512]{0,1:T(8,128)} %bitcast.2), channel_id=1, source_target_pairs={{16,0},{32,16},{48,32},{64,48},{80,64},{96,80},{112,96},{128,112},... | collective-permute-start | bytes 3145736 | tf_op jit(solution)/shard_map/ppermute | solution.py:15
  33.8 679.6 %copy-start.34 = (f32[6]{0:T(128)}, f32[6]{0:T(128)S(1)}, u32[]{:S(2)}) copy-start(f32[6]{0:T(128)S(1)} %bitcast_add_fusion.4) | copy-start | bytes 76
  33.9 10.5 collective-permute-start.9
  41.4 10.4 collective-permute-start.8
  162.6 217.2 %copy-start.29 = (f32[32]{0:T(128)}, f32[32]{0:T(128)S(1)}, u32[]{:S(2)}) copy-start(f32[32]{0:T(128)S(1)} %div.51) | copy-start | bytes 388
  165.9 528.8 %copy-start.7 = (f32[1,2,32,512]{3,2,1,0:T(8,128)S(1)}, f32[1,2,32,512]{3,2,1,0:T(8,128)}, u32[]{:S(2)}) copy-start(f32[1,2,32,512]{3,2,1,0:T(8,128)} %param.17) | copy-start | bytes 393220
  260.3 6.1 collective-permute-start.11
  262.5 4.9 collective-permute-start.10
  267.5 9.9 collective-permute-start.13
  272.5 10.5 collective-permute-start.12
  474.9 6.0 collective-permute-start.15
  477.1 4.9 collective-permute-start.14
  482.1 9.9 collective-permute-start.17
  487.4 10.5 collective-permute-start.16
  690.3 7.3 collective-permute-start.19
  692.5 5.1 collective-permute-start.18
  697.6 863.4 %copy-start.3 = (f32[1,1,512,512]{3,2,1,0:T(8,128)S(1)}, f32[1,1,512,512]{3,2,1,0:T(8,128)}, u32[]{:S(2)}) copy-start(f32[1,1,512,512]{3,2,1,0:T(8,128)} %get-tuple-element.127) | copy-start | bytes 3145732
  697.6 10.0 collective-permute-start.21
  702.6 10.6 collective-permute-start.20
  906.4 6.6 collective-permute-start.23
  908.3 4.9 collective-permute-start.22
  913.2 9.9 collective-permute-start.25
  918.1 10.4 collective-permute-start.24
  1121.9 5.0 collective-permute-start.27
  1124.0 4.9 collective-permute-start.26
  1128.9 9.9 collective-permute-start.29
  1134.3 10.5 collective-permute-start.28
  1337.9 4.9 collective-permute-start.31
  1340.1 4.9 collective-permute-start.30
  1345.0 9.9 collective-permute-start.33
  1350.4 10.5 collective-permute-start.32
  1554.0 8.3 collective-permute-start.35
  1556.2 9.5 collective-permute-start.34
  1558.4 164.2 %copy-start.30 = (f32[32]{0:T(128)S(1)}, f32[32]{0:T(128)}, u32[]{:S(2)}) copy-start(f32[32]{0:T(128)} %copy-done.29) | copy-start | bytes 388
  1558.4 164.2 %copy-start.32 = (f32[32]{0:T(128)S(1)}, f32[32]{0:T(128)}, u32[]{:S(2)}) copy-start(f32[32]{0:T(128)} %copy-done.31) | copy-start | bytes 388
  1562.4 468.4 %collective-permute-start.3 = (f32[32,512]{1,0:T(8,128)}, f32[32,512]{1,0:T(8,128)}, u32[]{:S(2)}, u32[]{:S(2)}) collective-permute-start(f32[32,512]{1,0:T(8,128)} %get-tuple-element.137), channel_id=1, source_target_pairs={{16,0},{32,16},{48,32},{64,48},{80,64},{96,80},{112,96},{128,112},... | collective-permute-start | bytes 196616 | tf_op jit(solution)/shard_map/ppermute | solution.py:15
  1565.8 9.5 collective-permute-start.37
  1575.3 10.4 collective-permute-start.36
  1585.7 454.7 %collective-permute-start.38 = (f32[512,512]{0,1:T(8,128)}, f32[512,512]{0,1:T(8,128)}, u32[]{:S(2)}, u32[]{:S(2)}) collective-permute-start(f32[512,512]{0,1:T(8,128)} %bitcast.92), channel_id=1, source_target_pairs={{0,1},{1,2},{2,3},{3,4},{4,5},{5,6},{6,7},{7,8},{8,9},{9,10},{10,1... | collective-permute-start | bytes 3145736 | tf_op jit(solution)/shard_map/ppermute | solution.py:15
  1723.2 451.8 %collective-permute-start.39 = (f32[32,512]{1,0:T(8,128)}, f32[32,512]{1,0:T(8,128)}, u32[]{:S(2)}, u32[]{:S(2)}) collective-permute-start(f32[32,512]{1,0:T(8,128)} %get-tuple-element.132), channel_id=1, source_target_pairs={{0,1},{1,2},{2,3},{3,4},{4,5},{5,6},{6,7},{7,8},{8,9},{9,10},{10,1... | collective-permute-start | bytes 196616 | tf_op jit(solution)/shard_map/ppermute | solution.py:15
  1867.2 315.0 %collective-permute-start.40 = (f32[512,512]{0,1:T(8,128)}, f32[512,512]{0,1:T(8,128)}, u32[]{:S(2)}, u32[]{:S(2)}) collective-permute-start(f32[512,512]{0,1:T(8,128)} %bitcast.538), channel_id=1, source_target_pairs={{1,0},{2,1},{3,2},{4,3},{5,4},{6,5},{7,6},{8,7},{9,8},{10,9},{11,1... | collective-permute-start | bytes 3145736 | tf_op jit(solution)/shard_map/ppermute | solution.py:15
  1876.9 440.0 %collective-permute-start.41 = (f32[32,512]{1,0:T(8,128)}, f32[32,512]{1,0:T(8,128)}, u32[]{:S(2)}, u32[]{:S(2)}) collective-permute-start(f32[32,512]{1,0:T(8,128)} %get-tuple-element.133), channel_id=1, source_target_pairs={{1,0},{2,1},{3,2},{4,3},{5,4},{6,5},{7,6},{8,7},{9,8},{10,9},{11,1... | collective-permute-start | bytes 196616 | tf_op jit(solution)/shard_map/ppermute | solution.py:15
  (31 other events, 933.8 us)
where the time goes:
time: 2340 us; the launch traced here: 2320 us
  blocking collectives  1490 us (64%)
  other arithmetic  485 us (21%)
  starting transfers between devices  159 us (7%)
  matrix products  65.3 us (3%)
  waiting for transfers between devices  58.6 us (3%)
  local copies, waits for them, and re-layouts  54.3 us (2%)
    psum x8, blocking collectives, squares(): return lax.psum(jnp.sum(values * values, axis=0), ('sx', 'sy'))  776 us
    psum x7, blocking collectives, shards(): curve = lax.psum(jnp.sum(direction * image, axis=0), ('sx', 'sy'))  713 us
    another operation x56, other arithmetic, face_average(): factor = jnp.linalg.cholesky(summed)  316 us
    another operation x9, other arithmetic, face_average(): jax.scipy.linalg.solve_triangular(factor, forward, lower=True, trans=1)  160 us
    ppermute x16, starting transfers between devices, with_halo(): lax.ppermute(head, axis, [((i + 1) % count, i) for i in range(ends)])  60.7 us
    ppermute x16, starting transfers between devices, with_halo(): lax.ppermute(tail, axis, [(i, (i + 1) % count) for i in range(ends)])  53.9 us
    ppermute x16, waiting for transfers between devices, with_halo(): lax.ppermute(tail, axis, [(i, (i + 1) % count) for i in range(ends)])  52.2 us
  transfers between devices with their start and end apart: 42, of which 16 were waited for; matrix products, arithmetic and copies ran while one was open for 25% of the time, Pallas kernels for 0%

commit v1 on v0

v1 whole, which is shorter than its diff:
```python
import functools

import jax
import jax.numpy as jnp
from jax import lax
from jax.experimental import pallas as pl
from jax.experimental.pallas import tpu as pltpu
from jax.sharding import PartitionSpec as P

CITERS = 8
HIGH = lax.Precision.HIGHEST
F = 512
R = 32
PC = 6
B = 128
PANELS = F // B
LIMIT = 56 * 2**20
MESH = pl.DeviceIdType.MESH
CX, CY, SH = 24, 64, 104


def dot(a, b, ca=1, cb=0):
    return lax.dot_general(
        a, b, (((ca,), (cb,)), ((), ())), precision=HIGH, preferred_element_type=jnp.float32
    )


def panel_copies(source, target, send, recv, device):
    return [
        pltpu.make_async_remote_copy(
            src_ref=source.at[pl.ds(k * B, B), pl.ds(k * B, F - k * B)],
            dst_ref=target.at[pl.ds(k * B, B), pl.ds(k * B, F - k * B)],
            send_sem=send.at[k],
            recv_sem=recv.at[k],
            device_id=device,
            device_id_type=MESH,
        )
        for k in range(PANELS)
    ]


def flat_row(block, first, stride, width):
    rows, cols = block.shape
    lane = lax.broadcasted_iota(jnp.int32, (cols, width), 1) - first
    hot = jnp.where(
        (lane >= 0) & (lane < stride * rows) & (lane % stride == lax.broadcasted_iota(jnp.int32, (cols, width), 0)),
        1.0,
        0.0,
    )
    spread = dot(block, hot)
    lane = lax.broadcasted_iota(jnp.int32, (rows, width), 1) - first
    own = (lane >= 0) & (lane // stride == lax.broadcasted_iota(jnp.int32, (rows, width), 0))
    return jnp.sum(jnp.where(own, spread, 0.0), axis=0, keepdims=True)


def b_row(b):
    parts = []
    for tile in range(2):
        lane = lax.broadcasted_iota(jnp.int32, (R, B), 1)
        column = 16 * tile + 4 * (lane // 32) + lane % 4
        hot = jnp.where(column == lax.broadcasted_iota(jnp.int32, (R, B), 0), 1.0, 0.0)
        spread = dot(b, hot)
        lane = lax.broadcasted_iota(jnp.int32, (PC, B), 1)
        own = (lane % 32) // 4 == lax.broadcasted_iota(jnp.int32, (PC, B), 0)
        parts.append(jnp.sum(jnp.where(own, spread, 0.0), axis=0, keepdims=True))
    return parts


def send_round(source_of, target, send, recv, mine, device_of):
    copies = []
    for d in range(1, 8):
        other = lax.rem(mine + d, 8)
        copies.append(
            pltpu.make_async_remote_copy(
                src_ref=source_of(other),
                dst_ref=target.at[mine],
                send_sem=send.at[d],
                recv_sem=recv.at[d],
                device_id=device_of(other),
                device_id_type=MESH,
            )
        )
    for copy in copies:
        copy.start()
    return copies


def rows8(values):
    return jnp.concatenate([values, values], axis=0)


def conjugate_gradients(table, nexts, diag, coarse, remain, search):
    nexts[0:40, :] = pltpu.roll(table[CX : CX + 40, :], F - 1, 1)
    nexts[40:80, :] = pltpu.roll(table[CY : CY + 40, :], F - 32, 1)

    def link(base, a, b):
        return jnp.broadcast_to(table[base + 6 * a + b : base + 6 * a + b + 1, :], (8, F))

    def beyond(base, a, b):
        return jnp.broadcast_to(nexts[base + 6 * a + b : base + 6 * a + b + 1, :], (8, F))

    for k in range(PC):
        total = jnp.broadcast_to(table[SH + k : SH + k + 1, :], (8, F))
        for a in range(PC):
            total += jnp.abs(link(CX, a, k)) + jnp.abs(link(CY, a, k))
            total += jnp.abs(beyond(0, k, a)) + jnp.abs(beyond(40, k, a))
        diag[8 * k : 8 * k + 8, :] = total
        start = rows8(table[4 * k : 4 * k + 4, :])
        coarse[8 * k : 8 * k + 8, :] = jnp.zeros((8, F), jnp.float32)
        remain[8 * k : 8 * k + 8, :] = start
        search[8 * k : 8 * k + 8, :] = start

    def total_of(left, right):
        product = left * right
        part = product[0:8]
        for k in range(1, PC):
            part += product[8 * k : 8 * k + 8]
        part = (part[:, 0:128] + part[:, 128:256]) + (part[:, 256:384] + part[:, 384:512])
        return jnp.broadcast_to(jnp.sum(part, axis=1, keepdims=True), (8, F))

    def sweep(step, now):
        p = search[...]
        low_x, high_x = pltpu.roll(p, 1, 1), pltpu.roll(p, F - 1, 1)
        low_y, high_y = pltpu.roll(p, 32, 1), pltpu.roll(p, F - 32, 1)
        images = []
        for k in range(PC):
            image = diag[8 * k : 8 * k + 8, :] * p[8 * k : 8 * k + 8]
            for a in range(PC):
                rows = slice(8 * a, 8 * a + 8)
                image += link(CX, a, k) * low_x[rows] + beyond(0, k, a) * high_x[rows]
                image += link(CY, a, k) * low_y[rows] + beyond(40, k, a) * high_y[rows]
            images.append(image)
        image = jnp.concatenate(images, axis=0)
        alpha = jnp.concatenate([now / total_of(p, image)] * PC, axis=0)
        coarse[...] += alpha * p
        left = remain[...] - alpha * image
        remain[...] = left
        new = total_of(left, left)
        search[...] = left + jnp.concatenate([new / now] * PC, axis=0) * p
        return new

    first = remain[...]
    lax.fori_loop(0, CITERS, sweep, total_of(first, first))


def exchange(
    schur_x, schur_y, residual_x, residual_y, basis_x, basis_y, couple_x, couple_y, shift,
    sum_x, sum_y, side_x, side_y, coarse_t,
    high_x, high_y, local_x, local_y, out_tx, out_ty, in_tx, in_ty,
    msg, near, plane, slabs, whole, table, nexts, diag, coarse, remain, search, back, home,
    load_sem, sx_send, sx_recv, sy_send, sy_recv, t_send, t_recv,
    a_send, a_recv, b_send, b_recv, c_send, c_recv, d_send, d_recv,
):
    i, j = lax.axis_index("sx"), lax.axis_index("sy")
    x_low, x_high = (lax.rem(i + 31, 32), j), (lax.rem(i + 1, 32), j)
    y_low, y_high = (i, lax.rem(j + 15, 16)), (i, lax.rem(j + 1, 16))
    q, y, z = lax.rem(i, 8), lax.rem(j, 2) * 4 + i // 8, j // 2

    def near_of(other):
        return ((i // 8) * 8 + other, j)

    def plane_of(other):
        return (lax.rem(other, 4) * 8 + q, z * 2 + other // 4)

    def stack_of(other):
        return (i, other * 2 + lax.rem(j, 2))

    loads = []
    for s, (source, target) in enumerate(
        ((schur_y.at[0, 0], local_y.at[0]), (schur_x.at[0, 0], local_x.at[0]),
         (schur_x.at[1, 0], local_x.at[1]), (schur_y.at[0, 1], local_y.at[1]))
    ):
        copy = pltpu.make_async_copy(source, target, load_sem.at[s])
        copy.start()
        loads.append(copy)

    barrier = pltpu.get_barrier_semaphore()
    for device in (x_low, x_high, y_low, y_high):
        pl.semaphore_signal(barrier, inc=1, device_id=device, device_id_type=MESH)
    for d in range(1, 8):
        for mine, device_of in ((q, near_of), (y, plane_of), (z, stack_of)):
            pl.semaphore_signal(
                barrier, inc=1, device_id=device_of(lax.rem(mine + d, 8)), device_id_type=MESH
            )
    pl.semaphore_wait(barrier, 25)

    blocks_y = panel_copies(schur_y.at[0, 0], high_y, sy_send, sy_recv, y_low)
    blocks_x = panel_copies(schur_x.at[0, 0], high_x, sx_send, sx_recv, x_low)
    for copy in blocks_y + blocks_x:
        copy.start()

    b = dot(basis_x[0, 0], residual_x[0, 0], 1, 1) + dot(basis_x[1, 0], residual_x[1, 0], 1, 1)
    b += dot(basis_y[0, 0], residual_y[0, 0], 1, 1) + dot(basis_y[0, 1], residual_y[0, 1], 1, 1)
    b_tiles = b_row(b)
    keep_x, keep_y = (i > 0).astype(jnp.float32), (j > 0).astype(jnp.float32)
    links = flat_row(couple_x[0, 0] * keep_x, CX, PC, B) + flat_row(couple_y[0, 0] * keep_y, CY, PC, B)
    links += flat_row(shift[0], SH, PC, B)
    row = jnp.concatenate(b_tiles + [links], axis=1)
    msg[...] = jnp.broadcast_to(row, (8, 3 * B))
    near[q] = msg[...]
    copies = send_round(lambda other: msg, near, a_send, a_recv, q, near_of)
    for copy in copies:
        copy.wait()
    sub = lax.broadcasted_iota(jnp.int32, (8, 3 * B), 0)
    rows = jnp.zeros((8, 3 * B), jnp.float32)
    for s in range(8):
        rows = jnp.where(sub == s, near[s], rows)
    plane[y] = rows
    copies = send_round(lambda other: plane.at[y], plane, b_send, b_recv, y, plane_of)

    loads[0].wait()
    out_ty[...] = dot(residual_y[0, 0], local_y[0])
    t_y = pltpu.make_async_remote_copy(
        src_ref=out_ty, dst_ref=in_ty, send_sem=t_send.at[0], recv_sem=t_recv.at[0],
        device_id=y_low, device_id_type=MESH,
    )
    t_y.start()
    loads[1].wait()
    out_tx[...] = dot(residual_x[0, 0], local_x[0])
    t_x = pltpu.make_async_remote_copy(
        src_ref=out_tx, dst_ref=in_tx, send_sem=t_send.at[1], recv_sem=t_recv.at[1],
        device_id=x_low, device_id_type=MESH,
    )
    t_x.start()

    for copy in copies:
        copy.wait()
    lane = lax.broadcasted_iota(jnp.int32, (64, B), 1)
    data = plane[...].reshape(64, 3 * B)
    for s in range(8):
        tile = data[:, B * (s // 4) : B * (s // 4) + B]
        if s % 4:
            tile = pltpu.roll(tile, B - 32 * (s % 4), 1)
        slabs[s] = jnp.where(lane < 24, tile, data[:, 2 * B : 3 * B])
    whole[z] = slabs[z]
    copies = send_round(lambda other: slabs.at[other], whole, c_send, c_recv, z, stack_of)

    loads[2].wait()
    side_x[...] = dot(residual_x[1, 0], local_x[1])
    loads[3].wait()
    side_y[...] = dot(residual_y[0, 1], local_y[1])

    for copy in copies:
        copy.wait()
    for s in range(4):
        table[:, s * B : s * B + B] = whole[2 * s : 2 * s + 2].reshape(B, B).T
    conjugate_gradients(table, nexts, diag, coarse, remain, search)

    lane = lax.broadcasted_iota(jnp.int32, (8, B), 1)
    place = y * 8 + q
    for s in range(4):
        first = jnp.zeros((8, B), jnp.float32)
        second = first
        for k in range(PC):
            part = pltpu.roll(coarse[8 * k : 8 * k + 8, s * B : s * B + B], B - place, 1)
            first = jnp.where(lane == k, jnp.broadcast_to(part[:, 0:1], (8, B)), first)
            second = jnp.where(lane == k, jnp.broadcast_to(part[:, 64:65], (8, B)), second)
        back[2 * s] = first
        back[2 * s + 1] = second
    home[z] = back[z]
    copies = send_round(lambda other: back.at[other], home, d_send, d_recv, z, stack_of)
    for copy in copies:
        copy.wait()
    sub = lax.broadcasted_iota(jnp.int32, (8, B), 0)
    for s in range(4):
        coarse_t[8 * s : 8 * s + 8, :] = jnp.where(sub < 4, home[2 * s], home[2 * s + 1])

    t_x.wait()
    side_x[...] += in_tx[...]
    for k, copy in enumerate(blocks_x):
        copy.wait()
        rows, cols = slice(k * B, k * B + B), slice(k * B, F)
        sum_x[rows, cols] = high_x[rows, cols] + local_x[1, rows, cols]
    t_y.wait()
    side_y[...] += in_ty[...]
    for k, copy in enumerate(blocks_y):
        copy.wait()
        rows, cols = slice(k * B, k * B + B), slice(k * B, F)
        sum_y[rows, cols] = high_y[rows, cols] + local_y[1, rows, cols]


def spread(values):
    return jnp.broadcast_to(values, (8, B))


def panel(tiles_of, at, lane, sub, ahead):
    heads = [tiles[0] for tiles in tiles_of]
    columns = [[spread(head[:, at + c : at + c + 1]) for c in range(8)] for head in heads]
    for c in range(8):
        here = sub == c
        for f in range(len(heads)):
            own = columns[f][c]
            inverse = 1.0 / spread(own[c : c + 1, :])
            fresh = []
            for d in range(8):
                if d == c:
                    fresh.append(jnp.where(here, inverse, -own * inverse))
                else:
                    row = spread(columns[f][d][c : c + 1, :]) * inverse
                    fresh.append(jnp.where(here, row, columns[f][d] - own * row))
            row = spread(heads[f][c : c + 1, :]) * inverse
            heads[f] = jnp.where(here, row, heads[f] - own * row)
            columns[f] = fresh
    inside = (lane >= at) & (lane < at + 8)
    results = []
    for f, tiles in enumerate(tiles_of):
        head = heads[f]
        for c in range(8):
            head = jnp.where(lane == at + c, columns[f][c], head)
        result = [head]
        for t in range(1, 1 + ahead):
            parts = [
                spread(tiles[t][:, at + c : at + c + 1]) * spread(head[c : c + 1, :])
                for c in range(8)
            ]
            total = ((parts[0] + parts[1]) + (parts[2] + parts[3])) + (
                (parts[4] + parts[5]) + (parts[6] + parts[7])
            )
            result.append(jnp.where(inside, 0.0, tiles[t]) - total)
        rest = jnp.concatenate(tiles[1 + ahead :], axis=0)
        update = dot(rest[:, at : at + 8], head)
        for t in range(1 + ahead, len(tiles)):
            row = (t - 1 - ahead) * 8
            result.append(jnp.where(inside, 0.0, tiles[t]) - update[row : row + 8, :])
        results.append(result)
    return results


def inverses(matrices, unroll=4, ahead=2):
    lane = lax.broadcasted_iota(jnp.int32, (8, B), 1)
    sub = lax.broadcasted_iota(jnp.int32, (8, B), 0)

    def body(step, carry):
        tiles_of = [list(tiles) for tiles in carry]
        for u in range(unroll):
            tiles_of = panel(tiles_of, 8 * u, lane, sub, ahead)
            tiles_of = [tiles[1:] + tiles[:1] for tiles in tiles_of]
        return tuple(
            tuple(pltpu.roll(tile, B - 8 * unroll, 1) for tile in tiles) for tiles in tiles_of
        )

    start = tuple(tuple(m[8 * t : 8 * t + 8, :] for t in range(B // 8)) for m in matrices)
    end = lax.fori_loop(0, B // 8 // unroll, body, start)
    return [jnp.concatenate(tiles, axis=0) for tiles in end]


def solve_faces(sums, sides, weights):
    for k in range(PANELS):
        own, rest = slice(k * B, k * B + B), slice(k * B + B, F)
        for a, side, w, inverse in zip(
            sums, sides, weights, inverses([a[own, own] for a in sums]), strict=True
        ):
            part = dot(side[:, own], inverse)
            if k < PANELS - 1:
                row = a[own, rest]
                weight = dot(inverse, row)
                w[own, rest] = weight
                for m in range(k + 1, PANELS):
                    at = (m - k - 1) * B
                    a[m * B : m * B + B, m * B :] -= dot(row[:, at : at + B], weight[:, at:], 0, 0)
                side[:, rest] -= dot(part, row)
            side[:, own] = part
    for k in range(PANELS - 2, -1, -1):
        own, rest = slice(k * B, k * B + B), slice(k * B + B, F)
        for side, w in zip(sides, weights, strict=True):
            side[:, own] -= dot(side[:, rest], w[own, rest], 1, 1)


def solve(sum_x, sum_y, side_x, side_y, face_x, face_y, work_x, work_y, weight_x, weight_y):
    for source, target in ((sum_x, work_x), (sum_y, work_y)):
        for k in range(PANELS):
            rows, cols = slice(k * B, k * B + B), slice(k * B, F)
            target[rows, cols] = source[rows, cols]
    face_x[...] = side_x[...]
    face_y[...] = side_y[...]
    solve_faces((work_x, work_y), (face_x, face_y), (weight_x, weight_y))


def lifted(coarse_t, basis):
    total = coarse_t[:, 0:1] * basis[0:1, :]
    for k in range(1, PC):
        total += coarse_t[:, k : k + 1] * basis[k : k + 1, :]
    return total


def finish(
    face_x, face_y, residual_x, residual_y, basis_x, basis_y, coarse_t,
    out_x, out_y, values, low_x, low_y, send, recv,
):
    i, j = lax.axis_index("sx"), lax.axis_index("sy")
    x_low, x_high = (lax.rem(i + 31, 32), j), (lax.rem(i + 1, 32), j)
    y_low, y_high = (i, lax.rem(j + 15, 16)), (i, lax.rem(j + 1, 16))
    barrier = pltpu.get_barrier_semaphore()
    for device in (x_low, x_high, y_low, y_high):
        pl.semaphore_signal(barrier, inc=1, device_id=device, device_id_type=MESH)
    pl.semaphore_wait(barrier, 4)
    copies = [
        pltpu.make_async_remote_copy(
            src_ref=source, dst_ref=target, send_sem=send.at[s], recv_sem=recv.at[s],
            device_id=device, device_id_type=MESH,
        )
        for s, (source, target, device) in enumerate(
            ((face_y, low_y, y_high), (face_x, low_x, x_high))
        )
    ]
    for copy in copies:
        copy.start()
    c = coarse_t[...]
    values[0, 0] = jnp.concatenate([c] * 4, axis=0).T[0:PC, 0:R]
    out_x[1, 0] = jnp.where(i == 31, residual_x[1, 0], face_x[...]) + lifted(c, basis_x[1, 0])
    out_y[0, 1] = jnp.where(j == 15, residual_y[0, 1], face_y[...]) + lifted(c, basis_y[0, 1])
    copies[1].wait()
    out_x[0, 0] = jnp.where(i == 0, residual_x[0, 0], low_x[...]) + lifted(c, basis_x[0, 0])
    copies[0].wait()
    out_y[0, 0] = jnp.where(j == 0, residual_y[0, 0], low_y[...]) + lifted(c, basis_y[0, 0])


def f32(*shape):
    return jax.ShapeDtypeStruct(shape, jnp.float32)


def vmem(*shape):
    return pltpu.VMEM(shape, jnp.float32)


HBM = pl.BlockSpec(memory_space=pl.ANY)
LOCAL = pl.BlockSpec(memory_space=pltpu.VMEM)


def shards(
    schur_x, schur_y, residual_x, residual_y, basis_x, basis_y, couple_x, couple_y, coarse_shift
):
    dma = pltpu.SemaphoreType.DMA
    sum_x, sum_y, side_x, side_y, coarse_t = pl.pallas_call(
        exchange,
        name="exchange",
        out_shape=(f32(F, F), f32(F, F), f32(R, F), f32(R, F), f32(R, B)),
        in_specs=[HBM] * 2 + [LOCAL] * 7,
        out_specs=(LOCAL,) * 5,
        scratch_shapes=[
            vmem(F, F), vmem(F, F), vmem(2, F, F), vmem(2, F, F),
            vmem(R, F), vmem(R, F), vmem(R, F), vmem(R, F),
            vmem(8, 3 * B), vmem(8, 8, 3 * B), vmem(8, 8, 3 * B), vmem(8, 64, B), vmem(8, 64, B),
            vmem(B, F), vmem(80, F), vmem(8 * PC, F), vmem(8 * PC, F), vmem(8 * PC, F),
            vmem(8 * PC, F), vmem(8, 8, B), vmem(8, 8, B),
            dma((4,)), dma((4,)), dma((4,)), dma((4,)), dma((4,)), dma((2,)), dma((2,)),
        ] + [dma((8,))] * 8,
        compiler_params=pltpu.CompilerParams(
            collective_id=0, has_side_effects=True, vmem_limit_bytes=LIMIT
        ),
    )(schur_x, schur_y, residual_x, residual_y, basis_x, basis_y, couple_x, couple_y, coarse_shift)
    face_x, face_y = pl.pallas_call(
        solve,
        name="solve",
        out_shape=(f32(R, F), f32(R, F)),
        in_specs=[LOCAL] * 4,
        out_specs=(LOCAL,) * 2,
        scratch_shapes=[vmem(F, F)] * 4,
        compiler_params=pltpu.CompilerParams(vmem_limit_bytes=LIMIT),
    )(sum_x, sum_y, side_x, side_y)
    return pl.pallas_call(
        finish,
        name="finish",
        out_shape=(f32(2, 1, R, F), f32(1, 2, R, F), f32(1, 1, PC, R)),
        in_specs=[LOCAL] * 7,
        out_specs=(LOCAL,) * 3,
        scratch_shapes=[vmem(R, F), vmem(R, F), dma((2,)), dma((2,))],
        compiler_params=pltpu.CompilerParams(
            collective_id=1, has_side_effects=True, vmem_limit_bytes=LIMIT
        ),
    )(face_x, face_y, residual_x, residual_y, basis_x, basis_y, coarse_t)


def solution(mesh):
    cells = P("sx", "sy", None, None)
    return jax.shard_map(
        shards,
        mesh=mesh,
        in_specs=(cells,) * 8 + (P("sx", "sy", None),),
        out_specs=(cells,) * 3,
        check_vma=False,
    )
```

time: 2340 us -> 133 us (0.06)
  the two profiles are of different devices: /device:TPU:66 before, /device:TPU:64 now
where the time goes in v1:
time: 133 us; the launch traced here: 132 us
  Pallas kernels  122 us (92%)
  local copies, waits for them, and re-layouts  9.66 us (7%)
    pallas_call x1, Pallas kernels, shards(): pl.pallas_call(exchange, name='exchange', out_shape=(f32(F, F), f32(F, F)...  75.6 us
    pallas_call x1, Pallas kernels, shards(): pl.pallas_call(solve, name='solve', out_shape=(f32(R, F), f32(R, F)), in_...  34.8 us
    pallas_call x1, Pallas kernels, shards(): pl.pallas_call(finish, name='finish', out_shape=(f32(2, 1, R, F), f32(1,...  11.6 us
    unnamed x6, local copies, waits for them, and re-layouts  8.4 us

profile of v1, /device:TPU:64, one launch (start us, length us, event | category | flops | bytes accessed | tf_op | source)
XLA Modules:
  0.0 132.3 jit_solution(6586678056754634059)
XLA Ops:
  0.6 1.3 copy.14.couple_x
  1.9 1.3 copy.15.couple_y
  3.2 1.4 %copy.12.basis_x = f32[2,1,6,512]{3,2,1,0:T(8,128)} copy(f32[2,1,6,512]{3,1,2,0:T(1,128)} %param.13) | data formatting | bytes 49152 | tf_op args[4]
  4.5 1.4 %copy.13.basis_y = f32[1,2,6,512]{3,2,1,0:T(8,128)} copy(f32[1,2,6,512]{3,1,2,0:T(2,128)} %param.14) | data formatting | bytes 49152 | tf_op args[5]
  5.9 75.6 %exchange.1 = (f32[512,512]{1,0:T(8,128)}, f32[512,512]{1,0:T(8,128)}, f32[32,512]{1,0:T(8,128)}, f32[32,512]{1,0:T(8,128)}, f32[32,128]{1,0:T(8,128)}) custom-call(f32[2,1,512,512]{3,2,1,0:T(8,128)} %schur_x.1, f32[1,2,512,512]{3,2,1,0:T(8,128)} %schur_y.1, f32[2,1,32,512]{3,2,1,0:T(8,128)} %residual_x.3, f32[1,2,32,512]{3,2,1,0:T(8,128)} %residual_y.3, ...), custom_call_target="tpu_custom_call" | custom-call | tf_op jit(solution)/shard_map/exchange/pallas_call | solution.py:434
  81.5 34.8 %solve.1 = (f32[32,512]{1,0:T(8,128)}, f32[32,512]{1,0:T(8,128)}) custom-call(f32[512,512]{1,0:T(8,128)} %get-tuple-element.10.sum_x, f32[512,512]{1,0:T(8,128)} %get-tuple-element.11.sum_y, f32[32,512]{1,0:T(8,128)} %get-tuple-element.12.side_x, f32[32,512]{1,0:T(8,128)} %get-tuple-element.13.side_y), custom_call_target="tpu_custom_call" | custom-call | tf_op jit(solution)/shard_map/solve/pallas_call | solution.py:452
  116.3 11.6 %finish.1 = (f32[2,1,32,512]{3,2,1,0:T(8,128)}, f32[1,2,32,512]{3,2,1,0:T(8,128)}, f32[1,1,6,32]{3,2,1,0:T(8,128)}) custom-call(f32[32,512]{1,0:T(8,128)} %get-tuple-element.14.face_x, f32[32,512]{1,0:T(8,128)} %get-tuple-element.15.face_y, f32[2,1,32,512]{3,2,1,0:T(8,128)} %residual_x.3, f32[1,2,32,512]{3,2,1,0:T(8,128)} %residual_y.3, ...), custom_call_target="tpu_custom_call" | custom-call | tf_op jit(solution)/shard_map/finish/pallas_call | solution.py:461
  127.9 1.3 copy.18
  129.2 1.6 %copy.21 = f32[2,1,32,512]{3,2,1,0:T(8,128)} copy(f32[2,1,32,512]{3,2,1,0:T(8,128)} %get-tuple-element.23) | data formatting | bytes 262144
  130.8 1.6 %copy.22 = f32[1,2,32,512]{3,2,1,0:T(8,128)} copy(f32[1,2,32,512]{3,2,1,0:T(8,128)} %get-tuple-element.24) | data formatting | bytes 262144

commit v2 on v1

v2 whole, which is shorter than its diff:
```python
import functools

import jax
import jax.numpy as jnp
from jax import lax
from jax.experimental import pallas as pl
from jax.experimental.pallas import tpu as pltpu
from jax.sharding import PartitionSpec as P

CITERS = 8
HIGH = lax.Precision.HIGHEST
F = 512
R = 32
PC = 6
B = 128
PANELS = F // B
LIMIT = 56 * 2**20
MESH = pl.DeviceIdType.MESH
CX, CY, SH = 24, 64, 104
BETWEEN = 2


def dot(a, b, ca=1, cb=0):
    return lax.dot_general(
        a, b, (((ca,), (cb,)), ((), ())), precision=HIGH, preferred_element_type=jnp.float32
    )


def panel_copies(source, target, send, recv, device):
    return [
        pltpu.make_async_remote_copy(
            src_ref=source.at[pl.ds(k * B, B), pl.ds(k * B, F - k * B)],
            dst_ref=target.at[pl.ds(k * B, B), pl.ds(k * B, F - k * B)],
            send_sem=send.at[k],
            recv_sem=recv.at[k],
            device_id=device,
            device_id_type=MESH,
        )
        for k in range(PANELS)
    ]


def flat_row(block, first, stride, width):
    rows, cols = block.shape
    lane = lax.broadcasted_iota(jnp.int32, (cols, width), 1) - first
    hot = jnp.where(
        (lane >= 0) & (lane < stride * rows) & (lane % stride == lax.broadcasted_iota(jnp.int32, (cols, width), 0)),
        1.0,
        0.0,
    )
    spread = dot(block, hot)
    lane = lax.broadcasted_iota(jnp.int32, (rows, width), 1) - first
    own = (lane >= 0) & (lane // stride == lax.broadcasted_iota(jnp.int32, (rows, width), 0))
    return jnp.sum(jnp.where(own, spread, 0.0), axis=0, keepdims=True)


def b_row(b):
    parts = []
    for tile in range(2):
        lane = lax.broadcasted_iota(jnp.int32, (R, B), 1)
        column = 16 * tile + 4 * (lane // 32) + lane % 4
        hot = jnp.where(column == lax.broadcasted_iota(jnp.int32, (R, B), 0), 1.0, 0.0)
        spread = dot(b, hot)
        lane = lax.broadcasted_iota(jnp.int32, (8, B), 1)
        own = (lane % 32) // 4 == lax.broadcasted_iota(jnp.int32, (8, B), 0)
        parts.append(jnp.sum(jnp.where(own, spread, 0.0), axis=0, keepdims=True))
    return parts


def send_round(source_of, target, send, recv, mine, device_of):
    copies = []
    for d in range(1, 8):
        other = lax.rem(mine + d, 8)
        copies.append(
            pltpu.make_async_remote_copy(
                src_ref=source_of(other),
                dst_ref=target.at[mine],
                send_sem=send.at[d],
                recv_sem=recv.at[d],
                device_id=device_of(other),
                device_id_type=MESH,
            )
        )
    for copy in copies:
        copy.start()
    return copies


def rows8(values):
    return jnp.concatenate([values, values], axis=0)


def conjugate_gradients(table, nexts, diag, coarse, remain, search):
    nexts[0:40, :] = pltpu.roll(table[CX : CX + 40, :], F - 1, 1)
    nexts[40:80, :] = pltpu.roll(table[CY : CY + 40, :], F - 32, 1)

    def link(base, a, b):
        return jnp.broadcast_to(table[base + 6 * a + b : base + 6 * a + b + 1, :], (8, F))

    def beyond(base, a, b):
        return jnp.broadcast_to(nexts[base + 6 * a + b : base + 6 * a + b + 1, :], (8, F))

    for k in range(PC):
        total = jnp.broadcast_to(table[SH + k : SH + k + 1, :], (8, F))
        for a in range(PC):
            total += jnp.abs(link(CX, a, k)) + jnp.abs(link(CY, a, k))
            total += jnp.abs(beyond(0, k, a)) + jnp.abs(beyond(40, k, a))
        diag[8 * k : 8 * k + 8, :] = total
        start = rows8(table[4 * k : 4 * k + 4, :])
        coarse[8 * k : 8 * k + 8, :] = jnp.zeros((8, F), jnp.float32)
        remain[8 * k : 8 * k + 8, :] = start
        search[8 * k : 8 * k + 8, :] = start

    def total_of(left, right):
        product = left * right
        part = product[0:8]
        for k in range(1, PC):
            part += product[8 * k : 8 * k + 8]
        part = (part[:, 0:128] + part[:, 128:256]) + (part[:, 256:384] + part[:, 384:512])
        return jnp.broadcast_to(jnp.sum(part, axis=1, keepdims=True), (8, F))

    def sweep(step, now):
        p = search[...]
        low_x, high_x = pltpu.roll(p, 1, 1), pltpu.roll(p, F - 1, 1)
        low_y, high_y = pltpu.roll(p, 32, 1), pltpu.roll(p, F - 32, 1)
        images = []
        for k in range(PC):
            image = diag[8 * k : 8 * k + 8, :] * p[8 * k : 8 * k + 8]
            for a in range(PC):
                rows = slice(8 * a, 8 * a + 8)
                image += link(CX, a, k) * low_x[rows] + beyond(0, k, a) * high_x[rows]
                image += link(CY, a, k) * low_y[rows] + beyond(40, k, a) * high_y[rows]
            images.append(image)
        image = jnp.concatenate(images, axis=0)
        alpha = jnp.concatenate([now / total_of(p, image)] * PC, axis=0)
        coarse[...] += alpha * p
        left = remain[...] - alpha * image
        remain[...] = left
        new = total_of(left, left)
        search[...] = left + jnp.concatenate([new / now] * PC, axis=0) * p
        return new

    first = remain[...]
    lax.fori_loop(0, CITERS, sweep, total_of(first, first))


def spread(values):
    return jnp.broadcast_to(values, (8, B))


def panel(tiles_of, at, lane, sub, ahead):
    heads = [tiles[0] for tiles in tiles_of]
    columns = [[spread(head[:, at + c : at + c + 1]) for c in range(8)] for head in heads]
    for c in range(8):
        here = sub == c
        for f in range(len(heads)):
            own = columns[f][c]
            inverse = 1.0 / spread(own[c : c + 1, :])
            fresh = []
            for d in range(8):
                if d == c:
                    fresh.append(jnp.where(here, inverse, -own * inverse))
                else:
                    row = spread(columns[f][d][c : c + 1, :]) * inverse
                    fresh.append(jnp.where(here, row, columns[f][d] - own * row))
            row = spread(heads[f][c : c + 1, :]) * inverse
            heads[f] = jnp.where(here, row, heads[f] - own * row)
            columns[f] = fresh
    inside = (lane >= at) & (lane < at + 8)
    results = []
    for f, tiles in enumerate(tiles_of):
        head = heads[f]
        for c in range(8):
            head = jnp.where(lane == at + c, columns[f][c], head)
        result = [head]
        for t in range(1, 1 + ahead):
            parts = [
                spread(tiles[t][:, at + c : at + c + 1]) * spread(head[c : c + 1, :])
                for c in range(8)
            ]
            total = ((parts[0] + parts[1]) + (parts[2] + parts[3])) + (
                (parts[4] + parts[5]) + (parts[6] + parts[7])
            )
            result.append(jnp.where(inside, 0.0, tiles[t]) - total)
        rest = jnp.concatenate(tiles[1 + ahead :], axis=0)
        update = dot(rest[:, at : at + 8], head)
        for t in range(1 + ahead, len(tiles)):
            row = (t - 1 - ahead) * 8
            result.append(jnp.where(inside, 0.0, tiles[t]) - update[row : row + 8, :])
        results.append(result)
    return results


def inverses(matrices, unroll=4, ahead=2):
    lane = lax.broadcasted_iota(jnp.int32, (8, B), 1)
    sub = lax.broadcasted_iota(jnp.int32, (8, B), 0)

    def body(step, carry):
        tiles_of = [list(tiles) for tiles in carry]
        for u in range(unroll):
            tiles_of = panel(tiles_of, 8 * u, lane, sub, ahead)
            tiles_of = [tiles[1:] + tiles[:1] for tiles in tiles_of]
        return tuple(
            tuple(pltpu.roll(tile, B - 8 * unroll, 1) for tile in tiles) for tiles in tiles_of
        )

    start = tuple(tuple(m[8 * t : 8 * t + 8, :] for t in range(B // 8)) for m in matrices)
    end = lax.fori_loop(0, B // 8 // unroll, body, start)
    return [jnp.concatenate(tiles, axis=0) for tiles in end]


def solve_faces(sums, highs, arrivals, sides, weights, between):
    for k in range(PANELS):
        own, rest = slice(k * B, k * B + B), slice(k * B + B, F)
        for a, high, copies in zip(sums, highs, arrivals, strict=True):
            copies[k].wait()
            a[own, k * B :] += high[own, k * B :]
        for a, side, w, inverse in zip(
            sums, sides, weights, inverses([a[own, own] for a in sums]), strict=True
        ):
            part = dot(side[:, own], inverse)
            if k < PANELS - 1:
                row = a[own, rest]
                weight = dot(inverse, row)
                w[own, rest] = weight
                for m in range(k + 1, PANELS):
                    at = (m - k - 1) * B
                    a[m * B : m * B + B, m * B :] -= dot(row[:, at : at + B], weight[:, at:], 0, 0)
                side[:, rest] -= dot(part, row)
            side[:, own] = part
        between(k)
    for k in range(PANELS - 2, -1, -1):
        own, rest = slice(k * B, k * B + B), slice(k * B + B, F)
        for side, w in zip(sides, weights, strict=True):
            side[:, own] -= dot(side[:, rest], w[own, rest], 1, 1)


def lifted(coarse_t, rows):
    total = coarse_t[:, 0:1] * rows[0]
    for k in range(1, PC):
        total += coarse_t[:, k : k + 1] * rows[k]
    return total


def apply(
    schur_x, schur_y, residual_x, residual_y, basis_x, basis_y, couple_x, couple_y, shift,
    out_x, out_y, values,
    high_x, high_y, local_x, local_y, weight_x, weight_y, side_x, side_y, low_x, low_y,
    out_tx, out_ty, in_tx, in_ty,
    msg, near, plane, slabs, whole, table, nexts, diag, coarse, remain, search, back, home,
    load_sem, sx_send, sx_recv, sy_send, sy_recv, t_send, t_recv, u_send, u_recv,
    a_send, a_recv, b_send, b_recv, c_send, c_recv, d_send, d_recv,
):
    i, j = lax.axis_index("sx"), lax.axis_index("sy")
    x_low, x_high = (lax.rem(i + 31, 32), j), (lax.rem(i + 1, 32), j)
    y_low, y_high = (i, lax.rem(j + 15, 16)), (i, lax.rem(j + 1, 16))
    q, y, z = lax.rem(i, 8), lax.rem(j, 2) * 4 + i // 8, j // 2

    def near_of(other):
        return ((i // 8) * 8 + other, j)

    def plane_of(other):
        return (lax.rem(other, 4) * 8 + q, z * 2 + other // 4)

    def stack_of(other):
        return (i, other * 2 + lax.rem(j, 2))

    loads = []
    for s, (source, target) in enumerate(
        ((schur_y.at[0, 0], local_y.at[0]), (schur_x.at[0, 0], local_x.at[0]),
         (schur_x.at[1, 0], local_x.at[1]), (schur_y.at[0, 1], local_y.at[1]))
    ):
        copy = pltpu.make_async_copy(source, target, load_sem.at[s])
        copy.start()
        loads.append(copy)

    barrier = pltpu.get_barrier_semaphore()
    for device in (x_low, x_high, y_low, y_high):
        pl.semaphore_signal(barrier, inc=1, device_id=device, device_id_type=MESH)
    for d in range(1, 8):
        for mine, device_of in ((q, near_of), (y, plane_of), (z, stack_of)):
            pl.semaphore_signal(
                barrier, inc=1, device_id=device_of(lax.rem(mine + d, 8)), device_id_type=MESH
            )
    pl.semaphore_wait(barrier, 25)

    blocks_y = panel_copies(schur_y.at[0, 0], high_y, sy_send, sy_recv, y_low)
    blocks_x = panel_copies(schur_x.at[0, 0], high_x, sx_send, sx_recv, x_low)
    blocks_y[0].start()
    blocks_x[0].start()

    def to_low(source, target, s, device):
        return pltpu.make_async_remote_copy(
            src_ref=source, dst_ref=target, send_sem=t_send.at[s], recv_sem=t_recv.at[s],
            device_id=device, device_id_type=MESH,
        )

    rows_x = [[basis_x[s, k] for k in range(PC)] for s in range(2)]
    rows_y = [[basis_y[0, k, s : s + 1, :] for k in range(PC)] for s in range(2)]
    pad = jnp.zeros((2, F), jnp.float32)
    b = jnp.zeros((8, R), jnp.float32)
    for rows, residual in (
        (rows_x[0], residual_x[0, 0]), (rows_x[1], residual_x[1, 0]),
        (rows_y[0], residual_y[0, 0]), (rows_y[1], residual_y[0, 1]),
    ):
        b += dot(jnp.concatenate(rows + [pad], axis=0), residual, 1, 1)
    b_tiles = b_row(b)
    keep_x, keep_y = (i > 0).astype(jnp.float32), (j > 0).astype(jnp.float32)
    link_x = jnp.concatenate([couple_x[0, a] for a in range(PC)], axis=0) * keep_x
    link_y = jnp.concatenate([couple_y[0, a] for a in range(PC)], axis=0) * keep_y
    links = flat_row(link_x, CX, PC, B) + flat_row(link_y, CY, PC, B) + flat_row(shift[0], SH, PC, B)
    msg[...] = jnp.broadcast_to(jnp.concatenate(b_tiles + [links], axis=1), (8, 3 * B))
    near[q] = msg[...]
    near_copies = send_round(lambda other: msg, near, a_send, a_recv, q, near_of)
    for copy in blocks_x[1:]:
        copy.start()

    loads[0].wait()
    out_ty[...] = dot(residual_y[0, 0], local_y[0])
    t_y = to_low(out_ty, in_ty, 0, y_low)
    t_y.start()
    loads[1].wait()
    out_tx[...] = dot(residual_x[0, 0], local_x[0])
    t_x = to_low(out_tx, in_tx, 1, x_low)
    t_x.start()

    for copy in near_copies:
        copy.wait()
    sub = lax.broadcasted_iota(jnp.int32, (8, 3 * B), 0)
    rows = jnp.zeros((8, 3 * B), jnp.float32)
    for s in range(8):
        rows = jnp.where(sub == s, near[s], rows)
    plane[y] = rows
    plane_copies = send_round(lambda other: plane.at[y], plane, b_send, b_recv, y, plane_of)
    for copy in blocks_y[1:]:
        copy.start()

    loads[2].wait()
    side_x[...] = dot(residual_x[1, 0], local_x[1])
    loads[3].wait()
    side_y[...] = dot(residual_y[0, 1], local_y[1])
    t_x.wait()
    side_x[...] += in_tx[...]
    t_y.wait()
    side_y[...] += in_ty[...]

    stack_copies = []

    def between(k):
        if k != BETWEEN:
            return
        for copy in plane_copies:
            copy.wait()
        lane = lax.broadcasted_iota(jnp.int32, (64, B), 1)
        data = plane[...].reshape(64, 3 * B)
        for s in range(8):
            tile = data[:, B * (s // 4) : B * (s // 4) + B]
            if s % 4:
                tile = pltpu.roll(tile, B - 32 * (s % 4), 1)
            slabs[s] = jnp.where(lane < 24, tile, data[:, 2 * B : 3 * B])
        whole[z] = slabs[z]
        stack_copies.extend(
            send_round(lambda other: slabs.at[other], whole, c_send, c_recv, z, stack_of)
        )

    solve_faces(
        (local_x.at[1], local_y.at[1]), (high_x, high_y), (blocks_x, blocks_y),
        (side_x, side_y), (weight_x, weight_y), between,
    )
    faces = [
        pltpu.make_async_remote_copy(
            src_ref=source, dst_ref=target, send_sem=u_send.at[s], recv_sem=u_recv.at[s],
            device_id=device, device_id_type=MESH,
        )
        for s, (source, target, device) in enumerate(
            ((side_y, low_y, y_high), (side_x, low_x, x_high))
        )
    ]
    for copy in faces:
        copy.start()

    for copy in stack_copies:
        copy.wait()
    for s in range(4):
        table[:, s * B : s * B + B] = whole[2 * s : 2 * s + 2].reshape(B, B).T
    conjugate_gradients(table, nexts, diag, coarse, remain, search)

    lane = lax.broadcasted_iota(jnp.int32, (8, B), 1)
    place = y * 8 + q
    for s in range(4):
        first = jnp.zeros((8, B), jnp.float32)
        second = first
        for k in range(PC):
            part = pltpu.roll(coarse[8 * k : 8 * k + 8, s * B : s * B + B], B - place, 1)
            first = jnp.where(lane == k, jnp.broadcast_to(part[:, 0:1], (8, B)), first)
            second = jnp.where(lane == k, jnp.broadcast_to(part[:, 64:65], (8, B)), second)
        back[2 * s] = first
        back[2 * s + 1] = second
    home[z] = back[z]
    home_copies = send_round(lambda other: back.at[other], home, d_send, d_recv, z, stack_of)
    for copy in home_copies:
        copy.wait()
    sub = lax.broadcasted_iota(jnp.int32, (8, B), 0)
    c = jnp.concatenate([jnp.where(sub < 4, home[2 * s], home[2 * s + 1]) for s in range(4)], axis=0)
    turned = jnp.concatenate([c] * 4, axis=0).T
    for k in range(PC):
        values[0, k] = turned[k : k + 1, 0:R]
    out_x[1, 0] = jnp.where(i == 31, residual_x[1, 0], side_x[...]) + lifted(c, rows_x[1])
    out_y[0, 1] = jnp.where(j == 15, residual_y[0, 1], side_y[...]) + lifted(c, rows_y[1])
    faces[1].wait()
    out_x[0, 0] = jnp.where(i == 0, residual_x[0, 0], low_x[...]) + lifted(c, rows_x[0])
    faces[0].wait()
    out_y[0, 0] = jnp.where(j == 0, residual_y[0, 0], low_y[...]) + lifted(c, rows_y[0])


def f32(*shape):
    return jax.ShapeDtypeStruct(shape, jnp.float32)


def vmem(*shape):
    return pltpu.VMEM(shape, jnp.float32)


HBM = pl.BlockSpec(memory_space=pl.ANY)
LOCAL = pl.BlockSpec(memory_space=pltpu.VMEM)


def shards(
    schur_x, schur_y, residual_x, residual_y, basis_x, basis_y, couple_x, couple_y, coarse_shift
):
    dma = pltpu.SemaphoreType.DMA

    def turn(array):
        return jnp.swapaxes(array, 1, 2)

    out_x, out_y, values = pl.pallas_call(
        apply,
        name="apply",
        out_shape=(f32(2, 1, R, F), f32(1, 2, R, F), f32(1, PC, 1, R)),
        in_specs=[HBM] * 2 + [LOCAL] * 7,
        out_specs=(LOCAL,) * 3,
        scratch_shapes=[
            vmem(F, F), vmem(F, F), vmem(2, F, F), vmem(2, F, F), vmem(F, F), vmem(F, F),
        ] + [vmem(R, F)] * 8 + [
            vmem(8, 3 * B), vmem(8, 8, 3 * B), vmem(8, 8, 3 * B), vmem(8, 64, B), vmem(8, 64, B),
            vmem(B, F), vmem(80, F), vmem(8 * PC, F), vmem(8 * PC, F), vmem(8 * PC, F),
            vmem(8 * PC, F), vmem(8, 8, B), vmem(8, 8, B),
            dma((4,)), dma((4,)), dma((4,)), dma((4,)), dma((4,)), dma((2,)), dma((2,)),
            dma((2,)), dma((2,)),
        ] + [dma((8,))] * 8,
        compiler_params=pltpu.CompilerParams(
            collective_id=0, has_side_effects=True, vmem_limit_bytes=LIMIT
        ),
    )(
        schur_x, schur_y, residual_x, residual_y,
        turn(basis_x), turn(basis_y), turn(couple_x), turn(couple_y), coarse_shift,
    )
    return out_x, out_y, turn(values)


def solution(mesh):
    cells = P("sx", "sy", None, None)
    return jax.shard_map(
        shards,
        mesh=mesh,
        in_specs=(cells,) * 8 + (P("sx", "sy", None),),
        out_specs=(cells,) * 3,
        check_vma=False,
    )
```

time: 133 us -> 101 us (0.76)
  Pallas kernels: 122 us -> 96.2 us
  local copies, waits for them, and re-layouts: 9.66 us -> 4.38 us
    pallas_call x3 -> x1, Pallas kernels: 122 us -> 96.2 us  [shards(): pl.pallas_call(apply, name='apply', out_shape=(f32(2, 1, R, F), f32(1, 2,...]
    unnamed x6 -> x3, local copies, waits for them, and re-layouts: 8.4 us -> 4.38 us
where the time goes in v2:
time: 101 us
  Pallas kernels  96.2 us (95%)
  local copies, waits for them, and re-layouts  4.38 us (4%)
    pallas_call x1, Pallas kernels, shards(): pl.pallas_call(apply, name='apply', out_shape=(f32(2, 1, R, F), f32(1, 2,...  96.2 us
    unnamed x3, local copies, waits for them, and re-layouts  4.38 us

profile of v2, /device:TPU:64, one launch (start us, length us, event | category | flops | bytes accessed | tf_op | source)
XLA Modules:
  0.0 101.3 jit_solution(5314783173402957200)
XLA Ops:
  0.6 96.2 %apply.1 = (f32[2,1,32,512]{3,2,1,0:T(8,128)}, f32[1,2,32,512]{3,2,1,0:T(8,128)}, f32[1,6,1,32]{3,2,1,0:T(1,128)}) custom-call(f32[2,1,512,512]{3,2,1,0:T(8,128)} %schur_x.1, f32[1,2,512,512]{3,2,1,0:T(8,128)} %schur_y.1, f32[2,1,32,512]{3,2,1,0:T(8,128)} %residual_x.1, f32[1,2,32,512]{3,2,1,0:T(8,128)} %residual_y.1, f32[2,6,1,512]{3,2,1,0:T(1,128)} %bitcast.7, ...), custom_call_target="tpu_custom_call" | custom-call | tf_op jit(solution)/shard_map/apply/pallas_call | solution.py:436
  96.9 1.6 %copy.16 = f32[2,1,32,512]{3,2,1,0:T(8,128)} copy(f32[2,1,32,512]{3,2,1,0:T(8,128)} %get-tuple-element.15) | data formatting | bytes 262144
  98.4 1.6 %copy.17 = f32[1,2,32,512]{3,2,1,0:T(8,128)} copy(f32[1,2,32,512]{3,2,1,0:T(8,128)} %get-tuple-element.16) | data formatting | bytes 262144
  100.0 1.2 %copy.18 = f32[1,1,6,32]{3,1,2,0:T(1,128)} copy(f32[1,1,6,32]{3,1,2,0:T(1,128)} %bitcast.11) | data formatting | bytes 1536

commit v3 on v2

--- a/solution.py
+++ b/solution.py
@@ -17,7 +17,7 @@
 LIMIT = 56 * 2**20
 MESH = pl.DeviceIdType.MESH
 CX, CY, SH = 24, 64, 104
-BETWEEN = 2
+SLABS_AFTER, COARSE_AFTER = 0, 1
 
 
 def dot(a, b, ca=1, cb=0):
@@ -148,64 +148,76 @@
     return jnp.broadcast_to(values, (8, B))
 
 
-def panel(tiles_of, at, lane, sub, ahead):
-    heads = [tiles[0] for tiles in tiles_of]
+def pivots(heads, at, lane, sub):
+    heads = list(heads)
     columns = [[spread(head[:, at + c : at + c + 1]) for c in range(8)] for head in heads]
     for c in range(8):
         here = sub == c
+        one = jnp.where(here, 1.0, 0.0)
         for f in range(len(heads)):
             own = columns[f][c]
             inverse = 1.0 / spread(own[c : c + 1, :])
-            fresh = []
-            for d in range(8):
-                if d == c:
-                    fresh.append(jnp.where(here, inverse, -own * inverse))
-                else:
-                    row = spread(columns[f][d][c : c + 1, :]) * inverse
-                    fresh.append(jnp.where(here, row, columns[f][d] - own * row))
-            row = spread(heads[f][c : c + 1, :]) * inverse
-            heads[f] = jnp.where(here, row, heads[f] - own * row)
-            columns[f] = fresh
-    inside = (lane >= at) & (lane < at + 8)
-    results = []
-    for f, tiles in enumerate(tiles_of):
-        head = heads[f]
+            scaled = (own - one) * inverse
+            columns[f] = [
+                jnp.where(here, inverse, -own * inverse)
+                if d == c
+                else columns[f][d] - scaled * spread(columns[f][d][c : c + 1, :])
+                for d in range(8)
+            ]
+            heads[f] = heads[f] - scaled * spread(heads[f][c : c + 1, :])
+    for f in range(len(heads)):
         for c in range(8):
-            head = jnp.where(lane == at + c, columns[f][c], head)
-        result = [head]
-        for t in range(1, 1 + ahead):
-            parts = [
-                spread(tiles[t][:, at + c : at + c + 1]) * spread(head[c : c + 1, :])
-                for c in range(8)
-            ]
-            total = ((parts[0] + parts[1]) + (parts[2] + parts[3])) + (
-                (parts[4] + parts[5]) + (parts[6] + parts[7])
-            )
-            result.append(jnp.where(inside, 0.0, tiles[t]) - total)
-        rest = jnp.concatenate(tiles[1 + ahead :], axis=0)
-        update = dot(rest[:, at : at + 8], head)
-        for t in range(1 + ahead, len(tiles)):
-            row = (t - 1 - ahead) * 8
-            result.append(jnp.where(inside, 0.0, tiles[t]) - update[row : row + 8, :])
-        results.append(result)
-    return results
-
-
-def inverses(matrices, unroll=4, ahead=2):
+            heads[f] = jnp.where(lane == at + c, columns[f][c], heads[f])
+    return heads
+
+
+def eliminated(tile, head, at, inside):
+    parts = [
+        spread(tile[:, at + c : at + c + 1]) * spread(head[c : c + 1, :]) for c in range(8)
+    ]
+    total = ((parts[0] + parts[1]) + (parts[2] + parts[3])) + (
+        (parts[4] + parts[5]) + (parts[6] + parts[7])
+    )
+    return jnp.where(inside, 0.0, tile) - total
+
+
+def sixteen(tiles_of, at, lane, sub):
+    rests = [jnp.concatenate(tiles[4:], axis=0) for tiles in tiles_of]
+    tiles_of = [list(tiles) for tiles in tiles_of]
+    for u in range(2):
+        first = at + 8 * u
+        heads = pivots([tiles[u] for tiles in tiles_of], first, lane, sub)
+        inside = (lane >= first) & (lane < first + 8)
+        for tiles, head in zip(tiles_of, heads, strict=True):
+            tiles[u] = head
+            for v in (1 - u, 2, 3):
+                tiles[v] = eliminated(tiles[v], head, first, inside)
+    inside = (lane >= at) & (lane < at + 16)
+    zero = jnp.zeros((8, B), jnp.float32)
+    for tiles, rest in zip(tiles_of, rests, strict=True):
+        heads = [zero] * (at // 8) + tiles[:2] + [zero] * (B // 8 - 2 - at // 8)
+        update = dot(rest, jnp.concatenate(heads, axis=0))
+        for t in range(4, B // 8):
+            row = (t - 4) * 8
+            tiles[t] = jnp.where(inside, 0.0, tiles[t]) - update[row : row + 8, :]
+    return tiles_of
+
+
+def inverses(matrices, unroll=4):
     lane = lax.broadcasted_iota(jnp.int32, (8, B), 1)
     sub = lax.broadcasted_iota(jnp.int32, (8, B), 0)
 
     def body(step, carry):
         tiles_of = [list(tiles) for tiles in carry]
         for u in range(unroll):
-            tiles_of = panel(tiles_of, 8 * u, lane, sub, ahead)
-            tiles_of = [tiles[1:] + tiles[:1] for tiles in tiles_of]
+            tiles_of = sixteen(tiles_of, 16 * u, lane, sub)
+            tiles_of = [tiles[2:] + tiles[:2] for tiles in tiles_of]
         return tuple(
-            tuple(pltpu.roll(tile, B - 8 * unroll, 1) for tile in tiles) for tiles in tiles_of
+            tuple(pltpu.roll(tile, B - 16 * unroll, 1) for tile in tiles) for tiles in tiles_of
         )
 
     start = tuple(tuple(m[8 * t : 8 * t + 8, :] for t in range(B // 8)) for m in matrices)
-    end = lax.fori_loop(0, B // 8 // unroll, body, start)
+    end = lax.fori_loop(0, B // 16 // unroll, body, start)
     return [jnp.concatenate(tiles, axis=0) for tiles in end]
 
 
@@ -346,8 +358,35 @@
 
     stack_copies = []
 
+    home_copies = []
+
+    def coarse_solve():
+        for copy in stack_copies:
+            copy.wait()
+        for s in range(4):
+            table[:, s * B : s * B + B] = whole[2 * s : 2 * s + 2].reshape(B, B).T
+        conjugate_gradients(table, nexts, diag, coarse, remain, search)
+
+        lane = lax.broadcasted_iota(jnp.int32, (8, B), 1)
+        place = y * 8 + q
+        for s in range(4):
+            first = jnp.zeros((8, B), jnp.float32)
+            second = first
+            for k in range(PC):
+                part = pltpu.roll(coarse[8 * k : 8 * k + 8, s * B : s * B + B], B - place, 1)
+                first = jnp.where(lane == k, jnp.broadcast_to(part[:, 0:1], (8, B)), first)
+                second = jnp.where(lane == k, jnp.broadcast_to(part[:, 64:65], (8, B)), second)
+            back[2 * s] = first
+            back[2 * s + 1] = second
+        home[z] = back[z]
+        home_copies.extend(
+            send_round(lambda other: back.at[other], home, d_send, d_recv, z, stack_of)
+        )
+
     def between(k):
-        if k != BETWEEN:
+        if k == COARSE_AFTER:
+            coarse_solve()
+        if k != SLABS_AFTER:
             return
         for copy in plane_copies:
             copy.wait()
@@ -379,25 +418,6 @@
     for copy in faces:
         copy.start()
 
-    for copy in stack_copies:
-        copy.wait()
-    for s in range(4):
-        table[:, s * B : s * B + B] = whole[2 * s : 2 * s + 2].reshape(B, B).T
-    conjugate_gradients(table, nexts, diag, coarse, remain, search)
-
-    lane = lax.broadcasted_iota(jnp.int32, (8, B), 1)
-    place = y * 8 + q
-    for s in range(4):
-        first = jnp.zeros((8, B), jnp.float32)
-        second = first
-        for k in range(PC):
-            part = pltpu.roll(coarse[8 * k : 8 * k + 8, s * B : s * B + B], B - place, 1)
-            first = jnp.where(lane == k, jnp.broadcast_to(part[:, 0:1], (8, B)), first)
-            second = jnp.where(lane == k, jnp.broadcast_to(part[:, 64:65], (8, B)), second)
-        back[2 * s] = first
-        back[2 * s + 1] = second
-    home[z] = back[z]
-    home_copies = send_round(lambda other: back.at[other], home, d_send, d_recv, z, stack_of)
     for copy in home_copies:
         copy.wait()
     sub = lax.broadcasted_iota(jnp.int32, (8, B), 0)
@@ -413,6 +433,17 @@
     out_y[0, 0] = jnp.where(j == 0, residual_y[0, 0], low_y[...]) + lifted(c, rows_y[0])
 
 
+def carry_out(from_x, from_y, from_c, to_x, to_y, to_c, sem):
+    copies = [
+        pltpu.make_async_copy(source, target, sem.at[s])
+        for s, (source, target) in enumerate(((from_x, to_x), (from_y, to_y), (from_c, to_c)))
+    ]
+    for copy in copies:
+        copy.start()
+    for copy in copies:
+        copy.wait()
+
+
 def f32(*shape):
     return jax.ShapeDtypeStruct(shape, jnp.float32)
 
@@ -433,10 +464,11 @@
     def turn(array):
         return jnp.swapaxes(array, 1, 2)
 
-    out_x, out_y, values = pl.pallas_call(
+    shapes = (f32(2, 1, R, F), f32(1, 2, R, F), f32(1, PC, 1, R))
+    results = pl.pallas_call(
         apply,
         name="apply",
-        out_shape=(f32(2, 1, R, F), f32(1, 2, R, F), f32(1, PC, 1, R)),
+        out_shape=shapes,
         in_specs=[HBM] * 2 + [LOCAL] * 7,
         out_specs=(LOCAL,) * 3,
         scratch_shapes=[
@@ -455,6 +487,14 @@
         schur_x, schur_y, residual_x, residual_y,
         turn(basis_x), turn(basis_y), turn(couple_x), turn(couple_y), coarse_shift,
     )
+    out_x, out_y, values = pl.pallas_call(
+        carry_out,
+        name="carry_out",
+        out_shape=shapes,
+        in_specs=[HBM] * 3,
+        out_specs=(HBM,) * 3,
+        scratch_shapes=[dma((3,))],
+    )(*results)
     return out_x, out_y, turn(values)
 
 

time: 101 us -> 99.2 us (0.982)
  the two profiles are of different devices: /device:TPU:64 before, /device:TPU:8 now
where the time goes in v3:
time: 99.2 us; the launch traced here: 99.1 us
  Pallas kernels  98.3 us (99%)
    pallas_call x1, Pallas kernels, shards(): pl.pallas_call(apply, name='apply', out_shape=shapes, in_specs=[HBM] * 2...  89.1 us
    pallas_call x1, Pallas kernels, shards(): pl.pallas_call(carry_out, name='carry_out', out_shape=shapes, in_specs=[H...  9.16 us

profile of v3, /device:TPU:8, one launch (start us, length us, event | category | flops | bytes accessed | tf_op | source)
XLA Modules:
  0.0 99.1 jit_solution(15227818820985949487)
XLA Ops:
  0.6 89.1 %apply.1 = (f32[2,1,32,512]{3,2,1,0:T(8,128)}, f32[1,2,32,512]{3,2,1,0:T(8,128)}, f32[1,6,1,32]{3,2,1,0:T(1,128)}) custom-call(f32[2,1,512,512]{3,2,1,0:T(8,128)} %schur_x.1, f32[1,2,512,512]{3,2,1,0:T(8,128)} %schur_y.1, f32[2,1,32,512]{3,2,1,0:T(8,128)} %residual_x.1, f32[1,2,32,512]{3,2,1,0:T(8,128)} %residual_y.1, f32[2,6,1,512]{3,2,1,0:T(1,128)} %bitcast.7, ...), custom_call_target="tpu_custom_call" | custom-call | tf_op jit(solution)/shard_map/apply/pallas_call | solution.py:468
  89.7 9.2 %carry_out.1 = (f32[2,1,32,512]{3,2,1,0:T(8,128)}, f32[1,2,32,512]{3,2,1,0:T(8,128)}, f32[1,6,1,32]{3,2,1,0:T(1,128)}) custom-call(f32[2,1,32,512]{3,2,1,0:T(8,128)} %get-tuple-element.9.from_x, f32[1,2,32,512]{3,2,1,0:T(8,128)} %get-tuple-element.10.from_y, f32[1,6,1,32]{3,2,1,0:T(1,128)} %get-tuple-element.11.from_c), custom_call_target="tpu_custom_call" | custom-call | tf_op jit(solution)/shard_map/carry_out/pallas_call | solution.py:490

commit v4 on v3

--- a/solution.py
+++ b/solution.py
@@ -27,17 +27,29 @@
 
 
 def panel_copies(source, target, send, recv, device):
-    return [
-        pltpu.make_async_remote_copy(
-            src_ref=source.at[pl.ds(k * B, B), pl.ds(k * B, F - k * B)],
-            dst_ref=target.at[pl.ds(k * B, B), pl.ds(k * B, F - k * B)],
-            send_sem=send.at[k],
-            recv_sem=recv.at[k],
-            device_id=device,
-            device_id_type=MESH,
-        )
-        for k in range(PANELS)
-    ]
+    copies = []
+    for k in range(PANELS):
+        for cols in (pl.ds(k * B, B), pl.ds(k * B + B, F - k * B - B)):
+            if cols.size:
+                part = (pl.ds(k * B, B), cols)
+                copies.append(
+                    pltpu.make_async_remote_copy(
+                        src_ref=source.at[part],
+                        dst_ref=target.at[part],
+                        send_sem=send.at[len(copies)],
+                        recv_sem=recv.at[len(copies)],
+                        device_id=device,
+                        device_id_type=MESH,
+                    )
+                )
+    return copies
+
+
+def start_if(flag, copies):
+    @pl.when(flag)
+    def _():
+        for copy in copies:
+            copy.start()
 
 
 def flat_row(block, first, stride, width):
@@ -221,15 +233,18 @@
     return [jnp.concatenate(tiles, axis=0) for tiles in end]
 
 
-def solve_faces(sums, highs, arrivals, sides, weights, between):
+def solve_faces(sums, highs, arrived, sides, weights, between):
     for k in range(PANELS):
         own, rest = slice(k * B, k * B + B), slice(k * B + B, F)
-        for a, high, copies in zip(sums, highs, arrivals, strict=True):
-            copies[k].wait()
-            a[own, k * B :] += high[own, k * B :]
-        for a, side, w, inverse in zip(
-            sums, sides, weights, inverses([a[own, own] for a in sums]), strict=True
-        ):
+        arrived(2 * k)
+        for a, high in zip(sums, highs, strict=True):
+            a[own, own] += high[own, own]
+        inverted = inverses([a[own, own] for a in sums])
+        if k < PANELS - 1:
+            arrived(2 * k + 1)
+            for a, high in zip(sums, highs, strict=True):
+                a[own, rest] += high[own, rest]
+        for a, side, w, inverse in zip(sums, sides, weights, inverted, strict=True):
             part = dot(side[:, own], inverse)
             if k < PANELS - 1:
                 row = a[own, rest]
@@ -298,8 +313,26 @@
 
     blocks_y = panel_copies(schur_y.at[0, 0], high_y, sy_send, sy_recv, y_low)
     blocks_x = panel_copies(schur_x.at[0, 0], high_x, sx_send, sx_recv, x_low)
-    blocks_y[0].start()
-    blocks_x[0].start()
+    send_x, send_y, take_x, take_y = i > 0, j > 0, i < 31, j < 15
+    start_if(send_y, blocks_y[:3])
+    start_if(send_x, blocks_x[:3])
+
+    @pl.when(i == 31)
+    def _():
+        high_x[...] = jnp.zeros((F, F), jnp.float32)
+
+    @pl.when(j == 15)
+    def _():
+        high_y[...] = jnp.zeros((F, F), jnp.float32)
+
+    def arrived(index):
+        @pl.when(take_x)
+        def _():
+            blocks_x[index].wait_recv()
+
+        @pl.when(take_y)
+        def _():
+            blocks_y[index].wait_recv()
 
     def to_low(source, target, s, device):
         return pltpu.make_async_remote_copy(
@@ -324,8 +357,7 @@
     msg[...] = jnp.broadcast_to(jnp.concatenate(b_tiles + [links], axis=1), (8, 3 * B))
     near[q] = msg[...]
     near_copies = send_round(lambda other: msg, near, a_send, a_recv, q, near_of)
-    for copy in blocks_x[1:]:
-        copy.start()
+    start_if(send_x, blocks_x[3:])
 
     loads[0].wait()
     out_ty[...] = dot(residual_y[0, 0], local_y[0])
@@ -344,8 +376,7 @@
         rows = jnp.where(sub == s, near[s], rows)
     plane[y] = rows
     plane_copies = send_round(lambda other: plane.at[y], plane, b_send, b_recv, y, plane_of)
-    for copy in blocks_y[1:]:
-        copy.start()
+    start_if(send_y, blocks_y[3:])
 
     loads[2].wait()
     side_x[...] = dot(residual_x[1, 0], local_x[1])
@@ -403,7 +434,7 @@
         )
 
     solve_faces(
-        (local_x.at[1], local_y.at[1]), (high_x, high_y), (blocks_x, blocks_y),
+        (local_x.at[1], local_y.at[1]), (high_x, high_y), arrived,
         (side_x, side_y), (weight_x, weight_y), between,
     )
     faces = [
@@ -429,19 +460,21 @@
     out_y[0, 1] = jnp.where(j == 15, residual_y[0, 1], side_y[...]) + lifted(c, rows_y[1])
     faces[1].wait()
     out_x[0, 0] = jnp.where(i == 0, residual_x[0, 0], low_x[...]) + lifted(c, rows_x[0])
+    for flag, blocks in ((send_x, blocks_x), (send_y, blocks_y)):
+
+        @pl.when(flag)
+        def _(blocks=blocks):
+            for copy in blocks:
+                copy.wait_send()
+
     faces[0].wait()
     out_y[0, 0] = jnp.where(j == 0, residual_y[0, 0], low_y[...]) + lifted(c, rows_y[0])
 
 
-def carry_out(from_x, from_y, from_c, to_x, to_y, to_c, sem):
-    copies = [
-        pltpu.make_async_copy(source, target, sem.at[s])
-        for s, (source, target) in enumerate(((from_x, to_x), (from_y, to_y), (from_c, to_c)))
-    ]
-    for copy in copies:
-        copy.start()
-    for copy in copies:
-        copy.wait()
+def carry_out(from_x, from_y, from_c, to_x, to_y, to_c):
+    to_x[...] = from_x[...]
+    to_y[...] = from_y[...]
+    to_c[...] = from_c[...]
 
 
 def f32(*shape):
@@ -477,7 +510,7 @@
             vmem(8, 3 * B), vmem(8, 8, 3 * B), vmem(8, 8, 3 * B), vmem(8, 64, B), vmem(8, 64, B),
             vmem(B, F), vmem(80, F), vmem(8 * PC, F), vmem(8 * PC, F), vmem(8 * PC, F),
             vmem(8 * PC, F), vmem(8, 8, B), vmem(8, 8, B),
-            dma((4,)), dma((4,)), dma((4,)), dma((4,)), dma((4,)), dma((2,)), dma((2,)),
+            dma((4,)), dma((7,)), dma((7,)), dma((7,)), dma((7,)), dma((2,)), dma((2,)),
             dma((2,)), dma((2,)),
         ] + [dma((8,))] * 8,
         compiler_params=pltpu.CompilerParams(
@@ -491,9 +524,8 @@
         carry_out,
         name="carry_out",
         out_shape=shapes,
-        in_specs=[HBM] * 3,
-        out_specs=(HBM,) * 3,
-        scratch_shapes=[dma((3,))],
+        in_specs=[LOCAL] * 3,
+        out_specs=(LOCAL,) * 3,
     )(*results)
     return out_x, out_y, turn(values)
 

time: 99.2 us -> 88.6 us (0.89)
  the two profiles are of different devices: /device:TPU:8 before, /device:TPU:7 now
where the time goes in v4:
time: 88.6 us; the launch traced here: 88.4 us
  Pallas kernels  87.8 us (99%)
    pallas_call x1, Pallas kernels, shards(): pl.pallas_call(apply, name='apply', out_shape=shapes, in_specs=[HBM] * 2...  86.1 us

profile of v4, /device:TPU:7, one launch (start us, length us, event | category | flops | bytes accessed | tf_op | source)
XLA Modules:
  0.0 88.4 jit_solution(2788752628247044890)
XLA Ops:
  0.6 86.1 %apply.1 = (f32[2,1,32,512]{3,2,1,0:T(8,128)}, f32[1,2,32,512]{3,2,1,0:T(8,128)}, f32[1,6,1,32]{3,2,1,0:T(1,128)}) custom-call(f32[2,1,512,512]{3,2,1,0:T(8,128)} %schur_x.1, f32[1,2,512,512]{3,2,1,0:T(8,128)} %schur_y.1, f32[2,1,32,512]{3,2,1,0:T(8,128)} %residual_x.1, f32[1,2,32,512]{3,2,1,0:T(8,128)} %residual_y.1, f32[2,6,1,512]{3,2,1,0:T(1,128)} %bitcast.7, ...), custom_call_target="tpu_custom_call" | custom-call | tf_op jit(solution)/shard_map/apply/pallas_call | solution.py:501
  86.7 1.7 %carry_out.1 = (f32[2,1,32,512]{3,2,1,0:T(8,128)}, f32[1,2,32,512]{3,2,1,0:T(8,128)}, f32[1,6,1,32]{3,2,1,0:T(1,128)}) custom-call(f32[2,1,32,512]{3,2,1,0:T(8,128)} %get-tuple-element.9.from_x, f32[1,2,32,512]{3,2,1,0:T(8,128)} %get-tuple-element.10.from_y, f32[1,6,1,32]{3,2,1,0:T(1,128)} %get-tuple-element.11.from_c), custom_call_target="tpu_custom_call" | custom-call | tf_op jit(solution)/shard_map/carry_out/pallas_call | solution.py:523
